TPU v7x, 512 devices: a whole 4x8x8 slice. The times are simulated.
512 devices in a mesh: leaf: 128 (over y, z, core), sub: 4 (over x).
Axes of the slice: x: 4, y: 8, z: 8, core: 2. Of those that a mesh axis runs over, the one named last changes fastest.
Arguments:
- points: float32 [524288, 64], P(('leaf', 'sub')), may hold values from -6 to 6
- charges: float32 [524288, 16], P(('leaf', 'sub')), may hold values from -4.5 to 5.5
- order: int32 [512, 1024], P(('leaf', 'sub')), may hold values from 0 to 1023, each once within a row
- neighbours: int32 [1024, 32], P(('leaf', 'sub')), may hold values from 0 to 1023, as said below
- neighbour_mask: int32 [1024, 32], P(('leaf', 'sub')), may hold values from 0 to 1, as said below
- leaf_skel: int32 [1024, 128], P(('leaf', 'sub')), may hold values from 0 to 511, as said below
- pair_skel: int32 [512, 128], P(('leaf', 'sub')), may hold values from 0 to 255, as said below
- upper_skel: int32 [512, 128], replicated, may hold values from 0 to 255, as said below
Outputs:
- potentials: float32 [524288, 16], P(('leaf', 'sub'))
Inputs may be any that keep to these rules, and one draw needn't show every extreme that they name: `order`: each row is a permutation of the rows of one device's block. `neighbours`: for a leaf of group g (leaves g * 8 to (g + 1) * 8 - 1), the live slots name distinct leaves of groups g - 1, g and g + 1; a padded slot names the leaf itself. `neighbour_mask`: at most 24 live slots in a list. `leaf_skel`: distinct entries in a row. `pair_skel`: distinct entries in a row. `upper_skel`: distinct entries in a row; rows 0 and 1 are not read.
All inputs are finite; a program needn't handle non-finite values.
Results may differ from a plain program's by a relative error of at most 0.0034.
Values may be sent and summed in bfloat16 or wider, within the bound.
A program may use at most 128 MiB of HBM per device.

v0:
```python
import jax
import jax.numpy as jnp
from jax import lax
from jax.sharding import PartitionSpec as P

highest = lax.Precision.HIGHEST


def extended(value, sides, width):
    for axis, dim in sides:
        size, length = (lax.axis_size(axis), value.shape[dim])
        up = [(i, (i + 1) % size) for i in range(size - 1)]
        down = [(j, i) for i, j in up]
        last = lax.slice_in_dim(value, length - width, length, axis=dim)
        first = lax.slice_in_dim(value, 0, width, axis=dim)
        before = lax.ppermute(last, axis, up)
        after = lax.ppermute(first, axis, down)
        value = jnp.concatenate([before, value, after], axis=dim)
    return value


def from_partner(block, axis, apart):
    count = lax.axis_size(axis)
    route = []
    for low in range(count):
        high = low | 1 << apart
        if high != low and high < count:
            route += [(low, high), (high, low)]
    return lax.ppermute(block, axis, route)


def kernel(left_pts, right_pts):
    left_sq = jnp.sum(jnp.square(left_pts.astype(jnp.float32)), axis=-1)
    right_sq = jnp.sum(jnp.square(right_pts.astype(jnp.float32)), axis=-1)
    inner = jnp.dot(left_pts, right_pts.T, preferred_element_type=jnp.float32)
    return jnp.exp(-2.0 / left_pts.shape[-1] * (left_sq[:, None] + right_sq[None, :] - 2.0 * inner))


def climb(node_pts, node_up, other, is_left, chosen, is_last, feature_dim):
    other_pts = other[:, :feature_dim].astype(jnp.bfloat16)
    other_up = other[:, feature_dim:]
    left_pts = jnp.where(is_left, node_pts, other_pts)
    right_pts = jnp.where(is_left, other_pts, node_pts)
    cross_mat = kernel(left_pts, right_pts)
    far_term = jnp.where(
        is_left,
        jnp.dot(cross_mat, other_up, precision=highest),
        jnp.dot(cross_mat.T, other_up, precision=highest),
    )
    if is_last:
        return (far_term, None, node_pts, node_up)
    children = jnp.concatenate([left_pts, right_pts], axis=0)
    child_up = jnp.concatenate(
        [jnp.where(is_left, node_up, other_up), jnp.where(is_left, other_up, node_up)], axis=0
    )
    parent_pts = jnp.take(children, chosen, axis=0)
    parent_mat = kernel(parent_pts, children)
    return (far_term, parent_mat, parent_pts, jnp.dot(parent_mat, child_up, precision=highest))


def shards(points, charges, order, neighbours, neighbour_mask, leaf_skel, pair_skel, upper_skel):
    feature_dim = points.shape[1]
    rhs_count = charges.shape[1]
    leaves_here = leaf_skel.shape[0]
    leaf_size = points.shape[0] // leaves_here
    skel_size = leaf_skel.shape[1]
    sub_count = lax.axis_size("sub")
    leaf_count = lax.axis_size("leaf")
    sub_index = lax.axis_index("sub")
    leaf_index = lax.axis_index("leaf")
    group_size = leaves_here * sub_count
    placement = order[0]
    tree_pts = jnp.take(points, placement, axis=0)
    tree_chg = jnp.take(charges, placement, axis=0)
    low_pts = tree_pts.astype(jnp.bfloat16)
    low_chg = tree_chg.astype(jnp.bfloat16)
    packed = jnp.concatenate([low_pts, low_chg], axis=1).reshape(
        leaves_here, leaf_size, feature_dim + rhs_count
    )
    gathered = lax.all_gather(packed, "sub", axis=0, tiled=True)
    window = extended(gathered, (("leaf", 0),), group_size)
    window_start = (leaf_index - 1) * group_size
    local_ids = neighbours - window_start
    slot_ids = jnp.arange(3 * group_size, dtype=jnp.int32)
    counts = jnp.sum(
        jnp.where(local_ids[:, :, None] == slot_ids[None, None, :], neighbour_mask[:, :, None], 0),
        axis=1,
    ).astype(jnp.float32)

    def window_term(block_index):
        piece = lax.dynamic_index_in_dim(window, block_index, 0, keepdims=False)
        weights = kernel(low_pts, piece[:, :feature_dim]).astype(jnp.bfloat16)
        contrib = jnp.dot(weights, piece[:, feature_dim:], preferred_element_type=jnp.float32)
        scales = jnp.repeat(
            lax.dynamic_index_in_dim(counts, block_index, 1, keepdims=False), leaf_size
        )
        return scales[:, None] * contrib

    def near_step(running, block_index):
        contrib = window_term(block_index)
        return (running + contrib, None)

    near_field, _ = lax.scan(
        near_step,
        jnp.zeros((leaves_here * leaf_size, rhs_count), jnp.float32),
        jnp.arange(3 * group_size, dtype=jnp.int32),
    )
    leaf_pts = low_pts.reshape(leaves_here, leaf_size, feature_dim)
    leaf_chg = tree_chg.reshape(leaves_here, leaf_size, rhs_count)
    skel_pts = jnp.take_along_axis(leaf_pts, leaf_skel[:, :, None], axis=1)
    leaf_mats = jax.vmap(kernel)(skel_pts, leaf_pts)
    leaf_up = jnp.einsum("nsl,nlr->nsr", leaf_mats, leaf_chg, precision=highest)
    leaf_cross = kernel(skel_pts[0], skel_pts[1])
    leaf_far0 = jnp.dot(leaf_cross, leaf_up[1], precision=highest)
    leaf_far1 = jnp.dot(leaf_cross.T, leaf_up[0], precision=highest)
    children = skel_pts.reshape(2 * skel_size, feature_dim)
    child_up = leaf_up.reshape(2 * skel_size, rhs_count)
    node_pts = jnp.take(children, pair_skel[0], axis=0)
    pair_mat = kernel(node_pts, children)
    node_up = jnp.dot(pair_mat, child_up, precision=highest)
    devices = leaf_count * sub_count
    device = leaf_index * sub_count + sub_index
    sub_bits = sub_count.bit_length() - 1
    leaf_bits = leaf_count.bit_length() - 1
    path = []
    level_step = 0
    for bit_number in range(sub_bits):
        node_packed = jnp.concatenate([node_pts.astype(jnp.float32), node_up], axis=1)
        other = from_partner(node_packed.astype(jnp.bfloat16), "sub", bit_number).astype(
            node_packed.dtype
        )
        is_left = sub_index >> bit_number & 1 == 0
        heap_row = devices + device >> level_step + 1
        chosen = lax.dynamic_index_in_dim(upper_skel, heap_row, 0, keepdims=False)
        far_term, parent_mat, node_pts, node_up = climb(
            node_pts, node_up, other, is_left, chosen, False, feature_dim
        )
        path.append((far_term, parent_mat, is_left))
        level_step += 1
    for bit_number in range(leaf_bits):
        node_packed = jnp.concatenate([node_pts.astype(jnp.float32), node_up], axis=1)
        other = from_partner(node_packed, "leaf", bit_number)
        is_left = leaf_index >> bit_number & 1 == 0
        heap_row = devices + device >> level_step + 1
        chosen = lax.dynamic_index_in_dim(upper_skel, heap_row, 0, keepdims=False)
        far_term, parent_mat, node_pts, node_up = climb(
            node_pts, node_up, other, is_left, chosen, bit_number + 1 == leaf_bits, feature_dim
        )
        path.append((far_term, parent_mat, is_left))
        level_step += 1
    down_term = path[-1][0]
    for far_term, parent_mat, is_left in reversed(path[:-1]):
        back_term = jnp.dot(parent_mat.T, down_term, precision=highest)
        down_term = far_term + jnp.where(is_left, back_term[:skel_size], back_term[skel_size:])
    back_term = jnp.dot(pair_mat.T, down_term, precision=highest)
    leaf_terms = jnp.stack(
        [leaf_far0 + back_term[:skel_size], leaf_far1 + back_term[skel_size:]], axis=0
    )
    far_field = jnp.einsum("nsl,nsr->nlr", leaf_mats, leaf_terms, precision=highest)
    tree_out = near_field + far_field.reshape(leaves_here * leaf_size, rhs_count)
    return jnp.zeros_like(tree_out).at[placement].set(tree_out)


def solution(mesh):
    placed = (
        P(("leaf", "sub"), None),
        P(("leaf", "sub"), None),
        P(("leaf", "sub"), None),
        P(("leaf", "sub"), None),
        P(("leaf", "sub"), None),
        P(("leaf", "sub"), None),
        P(("leaf", "sub"), None),
        P(),
    )
    return jax.shard_map(
        shards, mesh=mesh, in_specs=placed, out_specs=P(("leaf", "sub"), None), check_vma=False
    )
```

profile of v0, /device:TPU:40, one launch (start us, length us, event | category | flops | bytes accessed | tf_op | source)
XLA Modules:
  0.0 284.5 jit_solution(1972897193276930123)
XLA Ops:
  5.3 3.2 %gather_fusion = bf16[1024,64]{1,0:T(8,128)(2,1)S(1)} fusion(bf16[1024,64]{1,0:T(8,128)(2,1)S(1)} %copy.85, s32[1024]{0:T(1024)S(1)} %broadcast_clamp_fusion), kind=kCustom, calls=%fused_computation.9 | custom fusion | bytes 266240 | tf_op jit(solution)/shard_map/jit(_take)/gather | solution.py:73
  8.6 2.8 gather_fusion.1
  12.1 13.4 %all_gather.3 = bf16[8,512,80]{1,2,0:T(8,128)(2,1)S(1)} all-gather(bf16[2,512,80]{1,2,0:T(8,128)(2,1)S(1)} %copy.87), channel_id=1, replica_groups=mesh['leaf'=128,'sub'=4] {'sub'}, dimensions={0}, use_global_device_ids=true | all-gather | bytes 819200 | tf_op jit(solution)/shard_map/all_gather | solution.py:80
  27.4 9.6 %collective-permute-start.1 = (bf16[8,512,80]{1,2,0:T(8,128)(2,1)S(1)}, bf16[8,512,80]{1,2,0:T(8,128)(2,1)}, u32[]{:S(2)}, u32[]{:S(2)}) collective-permute-start(bf16[8,512,80]{1,2,0:T(8,128)(2,1)S(1)} %all_gather.3), channel_id=1, source_target_pairs={{4,0},{8,4},{12,8},{16,12},{20,16},{24,20},{28,24},{32,28},{36,32}... | collective-permute-start | bytes 1966088 | tf_op jit(solution)/shard_map/ppermute | solution.py:17
  50.7 3.4 %collective-permute-start.3 = (bf16[128,80]{0,1:T(8,128)(2,1)S(1)}, bf16[128,80]{0,1:T(8,128)(2,1)S(1)}, u32[]{:S(2)}, u32[]{:S(2)}) collective-permute-start(bf16[128,80]{0,1:T(8,128)(2,1)S(1)} %pad_maximum_fusion.18), channel_id=1, source_target_pairs={{0,2},{2,0},{1,3},{3,1},{4,6},{6,4},{5,7},{7,5},{8,10},{10,8},{9,1... | collective-permute-start | bytes 61448 | tf_op jit(solution)/shard_map/ppermute | solution.py:29
  55.0 2.8 collective-permute-done.3
  67.0 3.0 %collective-permute-done.5 = f32[128,80]{0,1:T(8,128)S(1)} collective-permute-done((f32[128,80]{0,1:T(8,128)S(1)}, f32[128,80]{0,1:T(8,128)S(1)}, u32[]{:S(2)}, u32[]{:S(2)}) %collective-permute-start.5) | collective-permute-done | bytes 40992 | tf_op jit(solution)/shard_map/ppermute | solution.py:29
  74.4 3.9 %collective-permute-done.6 = f32[128,80]{0,1:T(8,128)S(1)} collective-permute-done((f32[128,80]{0,1:T(8,128)S(1)}, f32[128,80]{0,1:T(8,128)S(1)}, u32[]{:S(2)}, u32[]{:S(2)}) %collective-permute-start.6) | collective-permute-done | bytes 40992 | tf_op jit(solution)/shard_map/ppermute | solution.py:29
  79.8 6.8 %collective-permute-start.7 = (f32[128,80]{0,1:T(8,128)S(1)}, f32[128,80]{0,1:T(8,128)S(1)}, u32[]{:S(2)}, u32[]{:S(2)}) collective-permute-start(f32[128,80]{0,1:T(8,128)S(1)} %pad_maximum_fusion.6), channel_id=1, source_target_pairs={{0,32},{32,0},{4,36},{36,4},{8,40},{40,8},{12,44},{44,12},{16,48},... | collective-permute-start | bytes 122888 | tf_op jit(solution)/shard_map/ppermute | solution.py:29
  87.6 2.4 collective-permute-done.7
  94.4 3.0 %collective-permute-done.8 = f32[128,80]{0,1:T(8,128)S(1)} collective-permute-done((f32[128,80]{0,1:T(8,128)S(1)}, f32[128,80]{0,1:T(8,128)S(1)}, u32[]{:S(2)}, u32[]{:S(2)}) %collective-permute-start.8) | collective-permute-done | bytes 40992 | tf_op jit(solution)/shard_map/ppermute | solution.py:29
  99.0 2.7 collective-permute-start.9
  102.7 3.1 %collective-permute-done.9 = f32[128,80]{0,1:T(8,128)S(1)} collective-permute-done((f32[128,80]{0,1:T(8,128)S(1)}, f32[128,80]{0,1:T(8,128)S(1)}, u32[]{:S(2)}, u32[]{:S(2)}) %collective-permute-start.9) | collective-permute-done | bytes 40992 | tf_op jit(solution)/shard_map/ppermute | solution.py:29
  114.9 6.9 %collective-permute-done.10 = f32[128,80]{1,0:T(8,128)S(1)} collective-permute-done((f32[128,80]{1,0:T(8,128)S(1)}, f32[128,80]{1,0:T(8,128)S(1)}, u32[]{:S(2)}, u32[]{:S(2)}) %collective-permute-start.10) | collective-permute-done | bytes 40992 | tf_op jit(solution)/shard_map/ppermute | solution.py:29
  135.3 144.0 %while.11 = (s32[]{:T(128)}, f32[1024,16]{0,1:T(8,128)}, s32[24]{0:T(128)S(1)}, f32[2,24]{0,1:T(8,128)}, bf16[1024,64]{1,0:T(8,128)(2,1)S(1)}, /*index=5*/bf16[2...) while((s32[]{:T(128)}, f32[1024,16]{0,1:T(8,128)}, s32[24]{0:T(128)S(1)}, ...), condition=%wide.region_4.5_spmd.clone, body=%wide.region_1.0_spmd.clone.sunk | while | flops 86850056 | bytes 1208501 | solution.py:103
  144.3 2.2 fusion.287
  150.3 2.2 fusion.287
  156.3 2.2 fusion.287
  162.4 2.2 fusion.287
  168.4 2.2 fusion.287
  174.4 2.2 fusion.287
  180.5 2.2 fusion.287
  204.6 2.2 fusion.287
  280.4 3.3 %scatter_custom_fusion = f32[1024,16]{1,0:T(8,128)S(1)} fusion(s32[1024]{0:T(1024)} %bitcast.210, f32[1024,16]{1,0:T(8,128)S(1)} %copy.112, f32[]{:T(128)} %constant.78.clone.1), kind=kCustom, calls=%fused_computation.144 | custom fusion | bytes 66048 | tf_op jit(solution)/shard_map/scatter | solution.py:161
  (467 shorter events, 148.4 us)
Async XLA Ops:
  11.4 25.7 %copy-start.27 = (s32[2,128]{1,0:T(2,128)S(1)}, s32[2,128]{1,0:T(2,128)}, u32[]{:S(2)}) copy-start(s32[2,128]{1,0:T(2,128)} %param.17) | copy-start | bytes 3076
  11.4 27.4 %copy-start.29 = (s32[1,128]{1,0:T(1,128)S(1)}, s32[1,128]{1,0:T(1,128)}, u32[]{:S(2)}) copy-start(s32[1,128]{1,0:T(1,128)} %param.18) | copy-start | bytes 1540
  11.6 28.2 %copy-start.17 = (s32[1,1024]{1,0:T(1,128)S(1)}, s32[1,1024]{1,0:T(1,128)}, u32[]{:S(2)}) copy-start(s32[1,1024]{1,0:T(1,128)} %param.14) | copy-start | bytes 12292
  25.5 108.4 %collective-permute-start = (bf16[8,512,80]{1,2,0:T(8,128)(2,1)S(1)}, bf16[8,512,80]{1,2,0:T(8,128)(2,1)S(1)}, u32[]{:S(2)}, u32[]{:S(2)}) collective-permute-start(bf16[8,512,80]{1,2,0:T(8,128)(2,1)S(1)} %all_gather.3), channel_id=1, source_target_pairs={{0,4},{4,8},{8,12},{12,16},{16,20},{20,24},{24,28},{28,32},{32,36}... | collective-permute-start | bytes 1966088 | tf_op jit(solution)/shard_map/ppermute | solution.py:16
  27.4 106.5 %collective-permute-start.1 = (bf16[8,512,80]{1,2,0:T(8,128)(2,1)S(1)}, bf16[8,512,80]{1,2,0:T(8,128)(2,1)}, u32[]{:S(2)}, u32[]{:S(2)}) collective-permute-start(bf16[8,512,80]{1,2,0:T(8,128)(2,1)S(1)} %all_gather.3), channel_id=1, source_target_pairs={{4,0},{8,4},{12,8},{16,12},{20,16},{24,20},{28,24},{32,28},{36,32}... | collective-permute-start | bytes 1966088 | tf_op jit(solution)/shard_map/ppermute | solution.py:17
  43.5 5.7 %collective-permute-start.2 = (bf16[128,80]{0,1:T(8,128)(2,1)S(1)}, bf16[128,80]{0,1:T(8,128)(2,1)S(1)}, u32[]{:S(2)}, u32[]{:S(2)}) collective-permute-start(bf16[128,80]{0,1:T(8,128)(2,1)S(1)} %pad_maximum_fusion.17), channel_id=1, source_target_pairs={{0,1},{1,0},{2,3},{3,2},{4,5},{5,4},{6,7},{7,6},{8,9},{9,8},{10,11... | collective-permute-start | bytes 61448 | tf_op jit(solution)/shard_map/ppermute | solution.py:29
  50.7 7.2 %collective-permute-start.3 = (bf16[128,80]{0,1:T(8,128)(2,1)S(1)}, bf16[128,80]{0,1:T(8,128)(2,1)S(1)}, u32[]{:S(2)}, u32[]{:S(2)}) collective-permute-start(bf16[128,80]{0,1:T(8,128)(2,1)S(1)} %pad_maximum_fusion.18), channel_id=1, source_target_pairs={{0,2},{2,0},{1,3},{3,1},{4,6},{6,4},{5,7},{7,5},{8,10},{10,8},{9,1... | collective-permute-start | bytes 61448 | tf_op jit(solution)/shard_map/ppermute | solution.py:29
  59.4 3.1 %collective-permute-start.4 = (f32[128,80]{0,1:T(8,128)S(1)}, f32[128,80]{0,1:T(8,128)S(1)}, u32[]{:S(2)}, u32[]{:S(2)}) collective-permute-start(f32[128,80]{0,1:T(8,128)S(1)} %pad_maximum_fusion.3), channel_id=1, source_target_pairs={{0,4},{4,0},{8,12},{12,8},{16,20},{20,16},{24,28},{28,24},{32,36},... | collective-permute-start | bytes 122888 | tf_op jit(solution)/shard_map/ppermute | solution.py:29
  64.1 5.9 %collective-permute-start.5 = (f32[128,80]{0,1:T(8,128)S(1)}, f32[128,80]{0,1:T(8,128)S(1)}, u32[]{:S(2)}, u32[]{:S(2)}) collective-permute-start(f32[128,80]{0,1:T(8,128)S(1)} %pad_maximum_fusion.4), channel_id=1, source_target_pairs={{0,8},{8,0},{4,12},{12,4},{16,24},{24,16},{20,28},{28,20},{32,40},... | collective-permute-start | bytes 122888 | tf_op jit(solution)/shard_map/ppermute | solution.py:29
  71.5 6.8 %collective-permute-start.6 = (f32[128,80]{0,1:T(8,128)S(1)}, f32[128,80]{0,1:T(8,128)S(1)}, u32[]{:S(2)}, u32[]{:S(2)}) collective-permute-start(f32[128,80]{0,1:T(8,128)S(1)} %pad_maximum_fusion.5), channel_id=1, source_target_pairs={{0,16},{16,0},{4,20},{20,4},{8,24},{24,8},{12,28},{28,12},{32,48},... | collective-permute-start | bytes 122888 | tf_op jit(solution)/shard_map/ppermute | solution.py:29
  79.8 10.2 %collective-permute-start.7 = (f32[128,80]{0,1:T(8,128)S(1)}, f32[128,80]{0,1:T(8,128)S(1)}, u32[]{:S(2)}, u32[]{:S(2)}) collective-permute-start(f32[128,80]{0,1:T(8,128)S(1)} %pad_maximum_fusion.6), channel_id=1, source_target_pairs={{0,32},{32,0},{4,36},{36,4},{8,40},{40,8},{12,44},{44,12},{16,48},... | collective-permute-start | bytes 122888 | tf_op jit(solution)/shard_map/ppermute | solution.py:29
  91.6 5.9 %collective-permute-start.8 = (f32[128,80]{0,1:T(8,128)S(1)}, f32[128,80]{0,1:T(8,128)S(1)}, u32[]{:S(2)}, u32[]{:S(2)}) collective-permute-start(f32[128,80]{0,1:T(8,128)S(1)} %pad_maximum_fusion.7), channel_id=1, source_target_pairs={{0,64},{64,0},{4,68},{68,4},{8,72},{72,8},{12,76},{76,12},{16,80},... | collective-permute-start | bytes 122888 | tf_op jit(solution)/shard_map/ppermute | solution.py:29
  99.0 6.8 %collective-permute-start.9 = (f32[128,80]{0,1:T(8,128)S(1)}, f32[128,80]{0,1:T(8,128)S(1)}, u32[]{:S(2)}, u32[]{:S(2)}) collective-permute-start(f32[128,80]{0,1:T(8,128)S(1)} %pad_maximum_fusion.8), channel_id=1, source_target_pairs={{0,128},{128,0},{4,132},{132,4},{8,136},{136,8},{12,140},{140,12},... | collective-permute-start | bytes 122888 | tf_op jit(solution)/shard_map/ppermute | solution.py:29
  107.4 18.5 %copy-start.23 = (f32[128,16]{0,1:T(8,128)S(1)}, f32[128,16]{0,1:T(8,128)}, u32[]{:S(2)}) copy-start(f32[128,16]{0,1:T(8,128)} %fusion.150) | copy-start | bytes 24580
  107.4 19.6 %copy-start.22 = (f32[128,16]{0,1:T(8,128)S(1)}, f32[128,16]{0,1:T(8,128)}, u32[]{:S(2)}) copy-start(f32[128,16]{0,1:T(8,128)} %fusion.153) | copy-start | bytes 24580
  107.4 20.7 %copy-start.21 = (f32[128,16]{0,1:T(8,128)S(1)}, f32[128,16]{0,1:T(8,128)}, u32[]{:S(2)}) copy-start(f32[128,16]{0,1:T(8,128)} %fusion.156) | copy-start | bytes 24580
  107.4 21.8 %copy-start.20 = (f32[128,16]{0,1:T(8,128)S(1)}, f32[128,16]{0,1:T(8,128)}, u32[]{:S(2)}) copy-start(f32[128,16]{0,1:T(8,128)} %fusion.159) | copy-start | bytes 24580
  107.4 23.0 %copy-start.7 = (f32[128,128]{1,0:T(8,128)S(1)}, f32[128,128]{1,0:T(8,128)}, u32[]{:S(2)}) copy-start(f32[128,128]{1,0:T(8,128)} %copy-done.6) | copy-start | bytes 196612
  107.4 23.0 %copy-start.19 = (f32[128,16]{0,1:T(8,128)S(1)}, f32[128,16]{0,1:T(8,128)}, u32[]{:S(2)}) copy-start(f32[128,16]{0,1:T(8,128)} %fusion.162) | copy-start | bytes 24580
  107.4 24.0 %copy-start.5 = (f32[128,128]{1,0:T(8,128)S(1)}, f32[128,128]{1,0:T(8,128)}, u32[]{:S(2)}) copy-start(f32[128,128]{1,0:T(8,128)} %copy-done.4) | copy-start | bytes 196612
  107.4 24.0 %copy-start.18 = (f32[128,16]{0,1:T(8,128)S(1)}, f32[128,16]{0,1:T(8,128)}, u32[]{:S(2)}) copy-start(f32[128,16]{0,1:T(8,128)} %fusion.165) | copy-start | bytes 24580
  107.5 25.1 %copy-start.3 = (f32[128,128]{1,0:T(8,128)S(1)}, f32[128,128]{1,0:T(8,128)}, u32[]{:S(2)}) copy-start(f32[128,128]{1,0:T(8,128)} %fusion.74) | copy-start | bytes 196612
  111.1 10.8 %collective-permute-start.10 = (f32[128,80]{1,0:T(8,128)S(1)}, f32[128,80]{1,0:T(8,128)S(1)}, u32[]{:S(2)}, u32[]{:S(2)}) collective-permute-start(f32[128,80]{1,0:T(8,128)S(1)} %pad_maximum_fusion.2), channel_id=1, source_target_pairs={{0,256},{256,0},{4,260},{260,4},{8,264},{264,8},{12,268},{268,12},... | collective-permute-start | bytes 122888 | tf_op jit(solution)/shard_map/ppermute | solution.py:29
  135.3 144.0 %copy-start.2 = (f32[2,2,8,512]{3,2,0,1:T(8,128)S(1)}, f32[2,2,8,512]{3,2,0,1:T(8,128)}, u32[]{:S(2)}) copy-start(f32[2,2,8,512]{3,2,0,1:T(8,128)} %copy.120) | copy-start | bytes 196612
  (17 other events, 125.4 us)
where the time goes:
time: 288 us; the launch traced here: 285 us
  matrix products  78.2 us (27%)
  local copies, waits for them, and re-layouts  61.2 us (21%)
  loops' own time  46.5 us (16%)
  starting transfers between devices  36.1 us (13%)
  waiting for transfers between devices  26.9 us (9%)
  other arithmetic  21.1 us (7%)
  blocking collectives  13.4 us (5%)
    dot_general x24, matrix products, window_term(): jnp.dot(weights, piece[:, feature_dim:], preferred_element_type=jnp.float32)  52.8 us
    another operation x1, loops' own time, shards(): lax.scan(near_step, jnp.zeros((leaves_here * leaf_size, rhs_count), jnp.f...  46.5 us
    ppermute x9, waiting for transfers between devices, from_partner(): return lax.ppermute(block, axis, route)  26.8 us
    ppermute x9, starting transfers between devices, from_partner(): return lax.ppermute(block, axis, route)  24.6 us
    squeeze x24, local copies, waits for them, and re-layouts, window_term(): lax.dynamic_index_in_dim(counts, block_index, 1, keepdims=False)  16.6 us
    dynamic_slice x24, local copies, waits for them, and re-layouts, shards(): lax.scan(near_step, jnp.zeros((leaves_here * leaf_size, rhs_count), jnp.f...  14.5 us
    all_gather x1, blocking collectives, shards(): gathered = lax.all_gather(packed, 'sub', axis=0, tiled=True)  13.4 us
    ppermute x1, starting transfers between devices, extended(): after = lax.ppermute(first, axis, down)  9.58 us
  transfers between devices with their start and end apart: 11, of which 9 were waited for; matrix products, arithmetic and copies ran while one was open for 16% of the time, Pallas kernels for 0%

commit v1 on v0

v1 whole, which is shorter than its diff:
```python
import functools

import jax
import jax.numpy as jnp
from jax import lax
from jax.experimental import pallas as pl
from jax.experimental.pallas import tpu as pltpu
from jax.sharding import PartitionSpec as P

F32 = jnp.float32
BF16 = jnp.bfloat16
MESH = pl.DeviceIdType.MESH
TN = (((0,), (0,)), ((), ()))
NT = (((1,), (1,)), ((), ()))
LOG2E = 1.4426950408889634

DIM = 64
AUG = 16
RHS = 16
PTS = 1024
SKEL = 128
HALF = PTS // 2
AUGD = DIM + AUG
WROWS = AUGD + RHS
NROWS = AUGD + 2 * RHS


def split2(value):
    high = value.astype(BF16)
    return high, (value - high.astype(F32)).astype(BF16)


def split3(value):
    high = value.astype(BF16)
    rest = value - high.astype(F32)
    mid = rest.astype(BF16)
    return high.astype(F32), mid.astype(F32), (rest - mid.astype(F32)).astype(BF16).astype(F32)


def augment(pts_f32, member):
    width = pts_f32.shape[1]
    n = -0.5 * jnp.sum(pts_f32 * pts_f32, axis=0, keepdims=True)
    hi, mid, lo = split3(n)
    row = lax.broadcasted_iota(jnp.int32, (AUG, width), 0)
    out = jnp.where(row == 0, hi, jnp.where(row == 1, mid, jnp.where(row == 2, lo, 0.0)))
    out = jnp.where(row == 3, member, out)
    return jnp.where((row >= 8) & (row < 11), 1.0, out)


def swapped(block):
    aug = block[DIM:AUGD].astype(F32)
    aug = jnp.concatenate([aug[8:], aug[:8]], axis=0).astype(BF16)
    return jnp.concatenate([block[:DIM], aug], axis=0)


def gauss(std, swp):
    scale = LOG2E * 4.0 / DIM
    inner = lax.dot_general(std, swp, TN, preferred_element_type=F32)
    return jnp.exp2(inner * scale)


def apply_mat(u_hi, u_lo, mat):
    k_hi, k_lo = split2(mat)
    n = u_hi.shape[0]
    both = jnp.dot(jnp.concatenate([u_hi, u_lo], axis=0), k_hi, preferred_element_type=F32)
    return both[:n] + both[n:] + jnp.dot(u_hi, k_lo, preferred_element_type=F32)


def onehot(sel, rows):
    at = lax.broadcasted_iota(jnp.int32, (rows, sel.shape[1]), 0)
    return jnp.where(at == sel, 1.0, 0.0).astype(BF16)


def body(
    y_size, z_size,
    pts_ref, chg_ref, order_ref, nbr_ref, msk_ref, lsk_ref, psk_ref, usk_ref,
    out_ref,
    win, own_swp, acc, cnt, tree, lvl4, lvl2, leaf_nodes, far, downs,
    wsend, wrecv, tsend, trecv,
):
    leaf = lax.axis_index("leaf")
    sub = lax.axis_index("sub")
    leaf_count = lax.axis_size("leaf")
    device = leaf * 4 + sub
    core = leaf % 2
    z = (leaf // 2) % z_size
    y = leaf // (2 * z_size)
    prev = (leaf + leaf_count - 1) % leaf_count
    nxt = (leaf + 1) % leaf_count
    partner = leaf + 1 - 2 * core

    def x_peer(step):
        return (leaf, (sub + step) % 4)

    def z_peer(step):
        return ((y * z_size + (z + step) % z_size) * 2 + core, sub)

    def y_peer(step):
        return ((((y + step) % y_size) * z_size + z) * 2 + core, sub)

    other_core = [(partner, (sub + step) % 4) for step in range(4)]
    beyond = (leaf + leaf_count - 1 + 2 * core) % leaf_count
    greet = [x_peer(s) for s in (1, 2, 3)] + other_core + [(beyond, sub)]
    greet += [z_peer(s) for s in range(1, z_size)] + [y_peer(s) for s in range(1, y_size)]
    barrier = pltpu.get_barrier_semaphore()
    for peer in greet:
        pl.semaphore_signal(barrier, inc=1, device_id=peer, device_id_type=MESH)

    order = order_ref[...]
    second = order[:, HALF:]
    hi_hot = onehot(second // 128, 8)
    lo_hot = onehot(second % 128, 128)
    grid = lax.dot_general(hi_hot, lo_hot, NT, preferred_element_type=F32)
    member = jnp.concatenate([grid[k : k + 1] for k in range(8)], axis=1)

    pts = pts_ref[...].astype(BF16)
    chg = chg_ref[...]
    chg_hi, chg_lo = split2(chg)
    win[4, 0:DIM] = pts
    win[4, DIM:AUGD] = augment(pts.astype(F32), member).astype(BF16)
    win[4, AUGD:WROWS] = chg_hi

    pl.semaphore_wait(barrier, len(greet))

    def window_copy(slot, target_slot, index, peer):
        return pltpu.make_async_remote_copy(
            src_ref=win.at[slot], dst_ref=win.at[target_slot],
            send_sem=wsend.at[index], recv_sem=wrecv.at[target_slot],
            device_id=peer, device_id_type=MESH,
        )

    sends = []
    for step in (1, 3, 2):
        sends.append(window_copy(4, 4 + (4 - step) % 4, step - 1, x_peer(step)))
    sends.append(window_copy(4, 8, 3, (prev, sub)))
    sends.append(window_copy(4, 0, 4, (nxt, sub)))
    for copy in sends:
        copy.start()

    def window_wait(slot):
        pltpu.make_async_copy(win.at[slot], win.at[slot], wrecv.at[slot]).wait()

    k = lax.broadcasted_iota(jnp.int32, (24, 32), 0)
    slot_k = k // 2
    ids = ((leaf + slot_k // 4 - 1) * 4 + (sub + slot_k % 4) % 4) * 2 + k % 2
    for own in range(2):
        hit = jnp.where(nbr_ref[own : own + 1, :] == ids, msk_ref[own : own + 1, :], 0)
        total = jnp.sum(hit.astype(F32), axis=1, keepdims=True)
        cnt[own] = jnp.broadcast_to(total, (24, 128))

    own_block = win[4, 0:AUGD]
    own_swp[...] = swapped(own_block)
    coarse = (order // 32).astype(F32)
    fine = (order % 32).astype(F32)
    for own in range(2):
        pick = onehot(lsk_ref[own : own + 1, :], HALF)
        part = slice(own * HALF, (own + 1) * HALF)
        place = jnp.concatenate([coarse[:, part], fine[:, part]], axis=0)
        place = jnp.concatenate([place, jnp.zeros((6, HALF), F32)], axis=0).astype(BF16)
        found = jnp.dot(place, pick, preferred_element_type=F32)
        where = (found[0:1] * 32.0 + found[1:2]).astype(jnp.int32)
        skel = jnp.dot(own_block, onehot(where, PTS), preferred_element_type=F32).astype(BF16)
        mine = member if own else 1.0 - member
        mat = gauss(own_block, swapped(skel))
        weights = apply_mat(
            (chg_hi.astype(F32) * mine).astype(BF16), (chg_lo.astype(F32) * mine).astype(BF16), mat
        )
        leaf_nodes[own, 0:AUGD] = skel
        u_hi, u_lo = split2(weights)
        leaf_nodes[own, AUGD : AUGD + RHS] = u_hi
        leaf_nodes[own, AUGD + RHS : NROWS] = u_lo

    def parent_of(left, right, sel):
        both = jnp.concatenate([left, right], axis=1)
        children = both[0:AUGD]
        chosen = jnp.dot(children, onehot(sel, 2 * SKEL), preferred_element_type=F32).astype(BF16)
        mat = gauss(children, swapped(chosen))
        u_hi, u_lo = split2(apply_mat(both[AUGD : AUGD + RHS], both[AUGD + RHS : NROWS], mat))
        return jnp.concatenate([chosen, u_hi, u_lo], axis=0)

    def cross(mine, other):
        mat = gauss(other[0:AUGD], swapped(mine))
        return apply_mat(other[AUGD : AUGD + RHS], other[AUGD + RHS : NROWS], mat)

    def down_mat(index, parent, child):
        k_hi, k_lo = split2(gauss(parent[0:AUGD], swapped(child)))
        downs[index, 0] = k_hi
        downs[index, 1] = k_lo

    def down(index, value):
        v_hi, v_lo = split2(value)
        both = jnp.dot(
            jnp.concatenate([v_hi, v_lo], axis=0), downs[index, 0], preferred_element_type=F32
        )
        return both[:RHS] + both[RHS:] + jnp.dot(v_hi, downs[index, 1], preferred_element_type=F32)

    place8 = [core * 4 + sub, z, y]
    tree[0, pl.ds(place8[0], 1)] = parent_of(leaf_nodes[0], leaf_nodes[1], psk_ref[...])[None]

    def tree_copies(stage):
        slot = place8[stage]
        if stage == 0:
            peers = [x_peer(s) for s in (1, 3, 2)] + other_core
        elif stage == 1:
            peers = [z_peer(s) for s in range(1, z_size)]
        else:
            peers = [y_peer(s) for s in range(1, y_size)]
        return [
            pltpu.make_async_remote_copy(
                src_ref=tree.at[stage, slot], dst_ref=tree.at[stage, slot],
                send_sem=tsend.at[stage, i], recv_sem=trecv.at[stage, slot],
                device_id=peer, device_id_type=MESH,
            )
            for i, peer in enumerate(peers)
        ]

    def tree_wait(stage):
        def one(step, carry):
            slot = (place8[stage] + step) % 8
            pltpu.make_async_copy(
                tree.at[stage, slot], tree.at[stage, slot], trecv.at[stage, slot]
            ).wait()
            return carry

        lax.fori_loop(1, 8, one, 0)

    tree_sends = [tree_copies(0)]
    for copy in tree_sends[0]:
        copy.start()

    relays = []
    for i, dx in enumerate((1, 3, 2)):
        window_wait(4 + dx)
        relays.append(window_copy(4 + dx, 8 + dx, 5 + 2 * i, (prev, sub)))
        relays.append(window_copy(4 + dx, dx, 6 + 2 * i, (nxt, sub)))
        relays[-2].start()
        relays[-1].start()

    acc[...] = jnp.zeros_like(acc)

    def near(slot):
        aug = win[slot, DIM:AUGD].astype(F32)
        group = aug[3:4]
        charge = win[slot, AUGD:WROWS].astype(F32)
        rows = []
        for own in range(2):
            c0 = cnt[own, pl.ds(2 * slot, 1), 0:1]
            c1 = cnt[own, pl.ds(2 * slot + 1, 1), 0:1]
            rows.append(charge * (c0 + (c1 - c0) * group))
        rows = jnp.concatenate(rows, axis=0).astype(BF16)
        mat = gauss(win[slot, 0:AUGD], own_swp[...]).astype(BF16)
        acc[...] += jnp.dot(rows, mat, preferred_element_type=F32)

    def level(stage):
        counts = {0: (256, 128, 64), 1: (32, 16, 8), 2: (4, 2, 0)}[stage]
        base = {0: device // 8, 1: device // 64, 2: 0 * device}[stage]
        me = place8[stage]
        for j in range(4):
            sel = usk_ref[pl.ds(counts[0] + base * 4 + j, 1), :]
            lvl4[stage, j] = parent_of(tree[stage, 2 * j], tree[stage, 2 * j + 1], sel)
        for j in range(2):
            sel = usk_ref[pl.ds(counts[1] + base * 2 + j, 1), :]
            lvl2[stage, j] = parent_of(lvl4[stage, 2 * j], lvl4[stage, 2 * j + 1], sel)
        if stage < 2:
            sel = usk_ref[pl.ds(counts[2] + base, 1), :]
            top = parent_of(lvl2[stage, 0], lvl2[stage, 1], sel)
            tree[stage + 1, pl.ds(place8[stage + 1], 1)] = top[None]
            tree_sends.append(tree_copies(stage + 1))
            for copy in tree_sends[-1]:
                copy.start()

    def path(stage):
        me = place8[stage]
        a, b, c = me, me // 2, me // 4
        node8, sib8 = tree[stage, a], tree[stage, a + 1 - 2 * (a % 2)]
        node4, sib4 = lvl4[stage, b], lvl4[stage, b + 1 - 2 * (b % 2)]
        node2, sib2 = lvl2[stage, c], lvl2[stage, 1 - c]
        far[3 * stage] = cross(node8, sib8)
        far[3 * stage + 1] = cross(node4, sib4)
        far[3 * stage + 2] = cross(node2, sib2)
        down_mat(3 * stage, node4, node8)
        down_mat(3 * stage + 1, node2, node4)
        if stage < 2:
            down_mat(3 * stage + 2, tree[stage + 1, place8[stage + 1]], node2)

    near(4)

    def group_block(i, carry):
        near(4 + i)
        return carry

    def side_block(i, carry):
        dx = (i // 2) + (i // 4) * (1 - 2 * ((i // 2) % 2))
        slot = dx + 8 * (i % 2)
        window_wait(slot)
        near(slot)
        return carry

    lax.fori_loop(1, 4, group_block, 0)
    tree_wait(0)
    level(0)
    path(0)
    lax.fori_loop(0, 4, side_block, 0)
    tree_wait(1)
    level(1)
    path(1)
    lax.fori_loop(4, 8, side_block, 0)
    tree_wait(2)
    level(2)
    path(2)

    value = far[8]
    for index in range(7, -1, -1):
        value = far[index] + down(index, value)
    node = tree[0, place8[0]]
    v_hi, v_lo = split2(value)
    for own in range(2):
        mat = gauss(node[0:AUGD], swapped(leaf_nodes[own]))
        term = cross(leaf_nodes[own], leaf_nodes[1 - own]) + apply_mat(v_hi, v_lo, mat)
        t_hi, t_lo = split2(term)
        mat = gauss(leaf_nodes[own, 0:AUGD], own_swp[...])
        acc[own * RHS : (own + 1) * RHS] += apply_mat(t_hi, t_lo, mat)

    mine = win[4, DIM:AUGD].astype(F32)[3:4]
    out_ref[...] = jnp.where(mine > 0.5, acc[RHS:], acc[:RHS])

    for copy in sends + relays:
        copy.wait_send()
    for group in tree_sends:
        for copy in group:
            copy.wait_send()


def shards(points, charges, order, neighbours, neighbour_mask, leaf_skel, pair_skel, upper_skel):
    call = pl.pallas_call(
        functools.partial(body, 8, 8),
        out_shape=jax.ShapeDtypeStruct((RHS, PTS), F32),
        in_specs=[pl.BlockSpec(memory_space=pltpu.VMEM)] * 8,
        out_specs=pl.BlockSpec(memory_space=pltpu.VMEM),
        scratch_shapes=[
            pltpu.VMEM((12, WROWS, PTS), BF16),
            pltpu.VMEM((AUGD, PTS), BF16),
            pltpu.VMEM((2 * RHS, PTS), F32),
            pltpu.VMEM((2, 24, 128), F32),
            pltpu.VMEM((3, 8, NROWS, SKEL), BF16),
            pltpu.VMEM((3, 4, NROWS, SKEL), BF16),
            pltpu.VMEM((3, 2, NROWS, SKEL), BF16),
            pltpu.VMEM((2, NROWS, SKEL), BF16),
            pltpu.VMEM((9, RHS, SKEL), F32),
            pltpu.VMEM((8, 2, SKEL, SKEL), BF16),
            pltpu.SemaphoreType.DMA((11,)),
            pltpu.SemaphoreType.DMA((12,)),
            pltpu.SemaphoreType.DMA((3, 7)),
            pltpu.SemaphoreType.DMA((3, 8)),
        ],
        compiler_params=pltpu.CompilerParams(
            collective_id=0, has_side_effects=True, vmem_limit_bytes=56 << 20
        ),
        name="krr_matvec",
    )
    out = call(
        points.T, charges.T, order, neighbours, neighbour_mask, leaf_skel, pair_skel, upper_skel
    )
    return out.T


def solution(mesh):
    placed = (P(("leaf", "sub"), None),) * 7 + (P(),)
    return jax.shard_map(
        shards, mesh=mesh, in_specs=placed, out_specs=P(("leaf", "sub"), None), check_vma=False
    )
```

time: 288 us -> 54.3 us (0.19)
  the two profiles are of different devices: /device:TPU:40 before, /device:TPU:2 now
where the time goes in v1:
time: 54.3 us; the launch traced here: 54.1 us
  Pallas kernels  52.6 us (97%)
  local copies, waits for them, and re-layouts  1.47 us (3%)
    pallas_call x1, Pallas kernels, shards(): call(points.T, charges.T, order, neighbours, neighbour_mask, leaf_skel, p...  52.6 us
    unnamed x1, local copies, waits for them, and re-layouts  1.47 us

profile of v1, /device:TPU:2, one launch (start us, length us, event | category | flops | bytes accessed | tf_op | source)
XLA Modules:
  0.0 54.1 jit_solution(997254386047179570)
XLA Ops:
  0.0 52.6 %krr_matvec.1 = f32[16,1024]{1,0:T(8,128)} custom-call(f32[64,1024]{1,0:T(8,128)} %bitcast.4, f32[16,1024]{1,0:T(8,128)} %bitcast.5, s32[1,1024]{1,0:T(1,128)} %order_ref.1, s32[2,32]{1,0:T(2,128)} %nbr_ref.1, s32[2,32]{1,0:T(2,128)} %msk_ref.1, s32[2,128]{1,0:T(2,128)} %lsk_ref.1, s32[1,128]{1,0:T(1,128)} %psk_ref.1, s32[512,128]{1,0:T(8,128)} %usk_ref.1), custom_call_target="tpu_custom_call" | custom-call | tf_op jit(solution)/shard_map/krr_matvec/pallas_call | solution.py:361
  52.6 1.5 %copy.10 = f32[1024,16]{0,1:T(8,128)} copy(f32[1024,16]{0,1:T(8,128)} %bitcast.3) | data formatting | bytes 131072

commit v2 on v1

v2 whole, which is shorter than its diff:
```python
import functools

import jax
import jax.numpy as jnp
from jax import lax
from jax.experimental import pallas as pl
from jax.experimental.pallas import tpu as pltpu
from jax.sharding import PartitionSpec as P

F32 = jnp.float32
BF16 = jnp.bfloat16
MESH = pl.DeviceIdType.MESH
TN = (((0,), (0,)), ((), ()))
NT = (((1,), (1,)), ((), ()))
LOG2E = 1.4426950408889634

DIM = 64
AUG = 16
RHS = 16
PTS = 1024
SKEL = 128
HALF = PTS // 2
AUGD = DIM + AUG
WROWS = AUGD + RHS
UROWS = 2 * RHS


def split2(value):
    high = value.astype(BF16)
    return high, (value - high.astype(F32)).astype(BF16)


def split3(value):
    high = value.astype(BF16)
    rest = value - high.astype(F32)
    mid = rest.astype(BF16)
    return high.astype(F32), mid.astype(F32), (rest - mid.astype(F32)).astype(BF16).astype(F32)


def augment(pts_f32, member):
    width = pts_f32.shape[1]
    n = -0.5 * jnp.sum(pts_f32 * pts_f32, axis=0, keepdims=True)
    hi, mid, lo = split3(n)
    row = lax.broadcasted_iota(jnp.int32, (AUG, width), 0)
    out = jnp.where(row == 0, hi, jnp.where(row == 1, mid, jnp.where(row == 2, lo, 0.0)))
    out = jnp.where(row == 3, member, out)
    return jnp.where((row >= 8) & (row < 11), 1.0, out)


def swapped(block):
    aug = block[DIM:AUGD].astype(F32)
    aug = jnp.concatenate([aug[8:], aug[:8]], axis=0).astype(BF16)
    return jnp.concatenate([block[:DIM], aug], axis=0)


def gauss(std, swp):
    scale = LOG2E * 4.0 / DIM
    inner = lax.dot_general(std, swp, TN, preferred_element_type=F32)
    return jnp.exp2(inner * scale)


def stack2(value):
    high, low = split2(value)
    return jnp.concatenate([high, low], axis=0)


def apply_mat(stacked, mat):
    both = jnp.dot(stacked, mat, preferred_element_type=F32)
    half = both.shape[0] // 2
    return both[:half] + both[half:]


def onehot(sel, rows):
    at = lax.broadcasted_iota(jnp.int32, (rows, sel.shape[1]), 0)
    return jnp.where(at == sel, 1.0, 0.0).astype(BF16)


def choose(points, sel):
    return jnp.dot(points, onehot(sel, points.shape[1]), preferred_element_type=F32).astype(BF16)


def body(
    y_size, z_size,
    pts_ref, chg_ref, order_ref, nbr_ref, msk_ref, lsk_ref, psk_ref, usk_ref,
    out_ref,
    win, own_swp, acc, cnt, tp, tu, n8, n4, n2, u4, u2, ups, crosses, downs, far, leaf_mats,
    wsend, wrecv, psend, precv, usend, urecv,
):
    leaf = lax.axis_index("leaf")
    sub = lax.axis_index("sub")
    leaf_count = lax.axis_size("leaf")
    device = leaf * 4 + sub
    core = leaf % 2
    z = (leaf // 2) % z_size
    y = leaf // (2 * z_size)
    prev = (leaf + leaf_count - 1) % leaf_count
    nxt = (leaf + 1) % leaf_count
    partner = leaf + 1 - 2 * core

    def x_peer(step):
        return (leaf, (sub + step) % 4)

    def z_peer(step):
        return ((y * z_size + (z + step) % z_size) * 2 + core, sub)

    def y_peer(step):
        return ((((y + step) % y_size) * z_size + z) * 2 + core, sub)

    other_core = [(partner, (sub + step) % 4) for step in (0, 1, 3, 2)]
    beyond = (leaf + leaf_count - 1 + 2 * core) % leaf_count
    stage_peers = [
        [x_peer(s) for s in (2, 1, 3)] + other_core,
        [z_peer(s) for s in (4, 3, 5, 2, 6, 1, 7)],
        [y_peer(s) for s in (4, 3, 5, 2, 6, 1, 7)],
    ]
    greet = stage_peers[2] + stage_peers[1] + stage_peers[0] + [(beyond, sub)]
    barrier = pltpu.get_barrier_semaphore()
    for peer in greet:
        pl.semaphore_signal(barrier, inc=1, device_id=peer, device_id_type=MESH)
    place8 = [core * 4 + sub, z, y]

    def tree_copies(buffer, send_sem, recv_sem, stage):
        slot = place8[stage]
        return [
            pltpu.make_async_remote_copy(
                src_ref=buffer.at[stage, slot], dst_ref=buffer.at[stage, slot],
                send_sem=send_sem.at[stage, i], recv_sem=recv_sem.at[stage, slot],
                device_id=peer, device_id_type=MESH,
            )
            for i, peer in enumerate(stage_peers[stage])
        ]

    tree_sends = []

    def tree_send(buffer, send_sem, recv_sem, stage):
        copies = tree_copies(buffer, send_sem, recv_sem, stage)
        for copy in copies:
            copy.start()
        tree_sends.extend(copies)

    def tree_wait(buffer, recv_sem, stage):
        for step in range(1, 8):
            slot = (place8[stage] + step) % 8
            pltpu.make_async_copy(
                buffer.at[stage, slot], buffer.at[stage, slot], recv_sem.at[stage, slot]
            ).wait()

    order = order_ref[...]
    pts = pts_ref[...].astype(BF16)
    own_aug = augment(pts.astype(F32), 0.0)
    own_std = jnp.concatenate([pts, own_aug.astype(BF16)], axis=0)
    coarse = (order // 32).astype(F32)
    fine = (order % 32).astype(F32)
    skels = []
    for own in range(2):
        part = slice(own * HALF, (own + 1) * HALF)
        place = jnp.concatenate([coarse[:, part], fine[:, part], jnp.zeros((6, HALF), F32)], axis=0)
        pick = onehot(lsk_ref[own : own + 1, :], HALF)
        found = jnp.dot(place.astype(BF16), pick, preferred_element_type=F32)
        where = (found[0:1] * 32.0 + found[1:2]).astype(jnp.int32)
        skels.append(choose(own_std, where))
    pair = jnp.concatenate(skels, axis=1)
    node = choose(pair, psk_ref[...])
    tp[0, pl.ds(place8[0], 1)] = node[None, 0:DIM]

    pl.semaphore_wait(barrier, len(greet))
    tree_send(tp, psend, precv, 0)

    second = order[:, HALF:]
    grid = lax.dot_general(
        onehot(second // 128, 8), onehot(second % 128, 128), NT, preferred_element_type=F32
    )
    member = jnp.concatenate([grid[k : k + 1] for k in range(8)], axis=1)
    chg_hi, chg_lo = split2(chg_ref[...])
    row = lax.broadcasted_iota(jnp.int32, (AUG, PTS), 0)
    win[4, 0:DIM] = pts
    win[4, DIM:AUGD] = jnp.where(row == 3, member, own_aug).astype(BF16)
    win[4, AUGD:WROWS] = chg_hi

    def window_copy(slot, target_slot, index, peer):
        return pltpu.make_async_remote_copy(
            src_ref=win.at[slot], dst_ref=win.at[target_slot],
            send_sem=wsend.at[index], recv_sem=wrecv.at[target_slot],
            device_id=peer, device_id_type=MESH,
        )

    sends = []
    for step in (1, 3, 2):
        sends.append(window_copy(4, 4 + (4 - step) % 4, step - 1, x_peer(step)))
    sends.append(window_copy(4, 8, 3, (prev, sub)))
    sends.append(window_copy(4, 0, 4, (nxt, sub)))
    for copy in sends:
        copy.start()

    def window_wait(slot):
        pltpu.make_async_copy(win.at[slot], win.at[slot], wrecv.at[slot]).wait()

    weights = []
    for own in range(2):
        mine = member if own else 1.0 - member
        masked = jnp.concatenate([chg_hi.astype(F32) * mine, chg_lo.astype(F32) * mine], axis=0)
        mat = gauss(own_std, swapped(skels[own])).astype(BF16)
        weights.append(stack2(apply_mat(masked.astype(BF16), mat)))
    pair_mat = gauss(pair, swapped(node)).astype(BF16)
    tu[0, pl.ds(place8[0], 1)] = stack2(
        apply_mat(jnp.concatenate(weights, axis=1), pair_mat)
    )[None]
    tree_send(tu, usend, urecv, 0)

    k = lax.broadcasted_iota(jnp.int32, (24, 32), 0)
    slot_k = k // 2
    ids = ((leaf + slot_k // 4 - 1) * 4 + (sub + slot_k % 4) % 4) * 2 + k % 2
    for own in range(2):
        hit = jnp.where(nbr_ref[own : own + 1, :] == ids, msk_ref[own : own + 1, :], 0)
        total = jnp.sum(hit.astype(F32), axis=1, keepdims=True)
        cnt[own] = jnp.broadcast_to(total, (24, 128))

    own_swp[...] = swapped(own_std)
    for own in range(2):
        leaf_mats[own, :, 0:PTS] = gauss(skels[own], own_swp[...]).astype(BF16)
        leaf_mats[own, :, PTS:] = gauss(node, swapped(skels[own])).astype(BF16)
        mat = gauss(skels[1 - own], swapped(skels[own])).astype(BF16)
        far[9 + own] = apply_mat(weights[1 - own], mat)

    acc[...] = jnp.zeros_like(acc)

    def near(slot):
        aug = win[slot, DIM:AUGD].astype(F32)
        group = aug[3:4]
        charge = win[slot, AUGD:WROWS].astype(F32)
        rows = []
        for own in range(2):
            c0 = cnt[own, pl.ds(2 * slot, 1), 0:1]
            c1 = cnt[own, pl.ds(2 * slot + 1, 1), 0:1]
            rows.append(charge * (c0 + (c1 - c0) * group))
        rows = jnp.concatenate(rows, axis=0).astype(BF16)
        mat = gauss(win[slot, 0:AUGD], own_swp[...]).astype(BF16)
        acc[...] += jnp.dot(rows, mat, preferred_element_type=F32)

    def select_stage(stage):
        firsts = [(256, 128, 64), (32, 16, 8), (4, 2, 0)][stage]
        base = [device // 8, device // 64, 0 * device][stage]
        tree_wait(tp, precv, stage)
        nodes = []
        for j in range(8):
            pts = tp[stage, j]
            nodes.append(
                jnp.concatenate([pts, augment(pts.astype(F32), 0.0).astype(BF16)], axis=0)
            )
            n8[stage, j] = nodes[-1]
        for depth, kept in ((0, n4), (1, n2), (2, None)):
            if depth == 2 and stage == 2:
                break
            count = len(nodes) // 2
            pairs = [jnp.concatenate(nodes[2 * j : 2 * j + 2], axis=1) for j in range(count)]
            nodes = []
            for j in range(count):
                sel = usk_ref[pl.ds(firsts[depth] + base * count + j, 1), :]
                nodes.append(choose(pairs[j], sel))
                if kept is not None:
                    kept[stage, j] = nodes[-1]
        if stage < 2:
            tp[stage + 1, pl.ds(place8[stage + 1], 1)] = nodes[0][None, 0:DIM]
            tree_send(tp, psend, precv, stage + 1)
            return nodes[0]
        return None

    def pair_of(buffer, stage, j):
        return jnp.concatenate([buffer[stage, 2 * j], buffer[stage, 2 * j + 1]], axis=1)

    def path_of(stage):
        a = place8[stage]
        b, c = a // 2, a // 4
        return (a, a + 1 - 2 * (a % 2)), (b, b + 1 - 2 * (b % 2)), (c, 1 - c)

    def matrices(stage, top):
        for j in range(4):
            ups[stage, j] = gauss(pair_of(n8, stage, j), swapped(n4[stage, j])).astype(BF16)
        for j in range(2):
            ups[stage, 4 + j] = gauss(pair_of(n4, stage, j), swapped(n2[stage, j])).astype(BF16)
        if top is not None:
            ups[stage, 6] = gauss(pair_of(n2, stage, 0), swapped(top)).astype(BF16)
        (a, a1), (b, b1), (c, c1) = path_of(stage)
        node8, node4, node2 = n8[stage, a], n4[stage, b], n2[stage, c]
        crosses[3 * stage] = gauss(n8[stage, a1], swapped(node8)).astype(BF16)
        crosses[3 * stage + 1] = gauss(n4[stage, b1], swapped(node4)).astype(BF16)
        crosses[3 * stage + 2] = gauss(n2[stage, c1], swapped(node2)).astype(BF16)
        downs[3 * stage] = gauss(node4, swapped(node8)).astype(BF16)
        downs[3 * stage + 1] = gauss(node2, swapped(node4)).astype(BF16)
        if top is not None:
            downs[3 * stage + 2] = gauss(top, swapped(node2)).astype(BF16)

    def weights_stage(stage):
        tree_wait(tu, urecv, stage)
        for j in range(4):
            u4[stage, j] = stack2(apply_mat(pair_of(tu, stage, j), ups[stage, j]))
        for j in range(2):
            u2[stage, j] = stack2(apply_mat(pair_of(u4, stage, j), ups[stage, 4 + j]))
        if stage < 2:
            top = stack2(apply_mat(pair_of(u2, stage, 0), ups[stage, 6]))
            tu[stage + 1, pl.ds(place8[stage + 1], 1)] = top[None]
            tree_send(tu, usend, urecv, stage + 1)
        (a, a1), (b, b1), (c, c1) = path_of(stage)
        far[3 * stage] = apply_mat(tu[stage, a1], crosses[3 * stage])
        far[3 * stage + 1] = apply_mat(u4[stage, b1], crosses[3 * stage + 1])
        far[3 * stage + 2] = apply_mat(u2[stage, c1], crosses[3 * stage + 2])

    near(4)
    top = select_stage(0)
    matrices(0, top)
    weights_stage(0)

    relays = []
    for i, dx in enumerate((1, 3, 2)):
        window_wait(4 + dx)
        relays.append(window_copy(4 + dx, 8 + dx, 5 + 2 * i, (prev, sub)))
        relays.append(window_copy(4 + dx, dx, 6 + 2 * i, (nxt, sub)))
        relays[-2].start()
        relays[-1].start()

    def group_block(i, carry):
        near(4 + i)
        return carry

    def gray(i):
        return i + (i // 2) * (1 - 2 * (i % 2))

    def partner_block(i, carry):
        slot = gray(i) + 8 * (1 - core)
        window_wait(slot)
        near(slot)
        return carry

    def beyond_block(i, carry):
        slot = gray(i) + 8 * core
        window_wait(slot)
        near(slot)
        return carry

    lax.fori_loop(1, 4, group_block, 0)
    lax.fori_loop(0, 4, partner_block, 0)
    top = select_stage(1)
    matrices(1, top)
    weights_stage(1)
    lax.fori_loop(0, 4, beyond_block, 0)
    select_stage(2)
    matrices(2, None)
    weights_stage(2)

    value = far[8]
    for index in range(7, -1, -1):
        value = far[index] + apply_mat(stack2(value), downs[index])
    for own in range(2):
        term = far[9 + own] + apply_mat(stack2(value), leaf_mats[own, :, PTS:])
        acc[own * RHS : (own + 1) * RHS] += apply_mat(stack2(term), leaf_mats[own, :, 0:PTS])

    mine = win[4, DIM:AUGD].astype(F32)[3:4]
    out_ref[...] = jnp.where(mine > 0.5, acc[RHS:], acc[:RHS])

    for copy in sends + relays + tree_sends:
        copy.wait_send()


def shards(points, charges, order, neighbours, neighbour_mask, leaf_skel, pair_skel, upper_skel):
    call = pl.pallas_call(
        functools.partial(body, 8, 8),
        out_shape=jax.ShapeDtypeStruct((RHS, PTS), F32),
        in_specs=[pl.BlockSpec(memory_space=pltpu.VMEM)] * 8,
        out_specs=pl.BlockSpec(memory_space=pltpu.VMEM),
        scratch_shapes=[
            pltpu.VMEM((12, WROWS, PTS), BF16),
            pltpu.VMEM((AUGD, PTS), BF16),
            pltpu.VMEM((2 * RHS, PTS), F32),
            pltpu.VMEM((2, 24, 128), F32),
            pltpu.VMEM((3, 8, DIM, SKEL), BF16),
            pltpu.VMEM((3, 8, UROWS, SKEL), BF16),
            pltpu.VMEM((3, 8, AUGD, SKEL), BF16),
            pltpu.VMEM((3, 4, AUGD, SKEL), BF16),
            pltpu.VMEM((3, 2, AUGD, SKEL), BF16),
            pltpu.VMEM((3, 4, UROWS, SKEL), BF16),
            pltpu.VMEM((3, 2, UROWS, SKEL), BF16),
            pltpu.VMEM((3, 7, 2 * SKEL, SKEL), BF16),
            pltpu.VMEM((9, SKEL, SKEL), BF16),
            pltpu.VMEM((8, SKEL, SKEL), BF16),
            pltpu.VMEM((11, RHS, SKEL), F32),
            pltpu.VMEM((2, SKEL, PTS + SKEL), BF16),
            pltpu.SemaphoreType.DMA((11,)),
            pltpu.SemaphoreType.DMA((12,)),
            pltpu.SemaphoreType.DMA((3, 7)),
            pltpu.SemaphoreType.DMA((3, 8)),
            pltpu.SemaphoreType.DMA((3, 7)),
            pltpu.SemaphoreType.DMA((3, 8)),
        ],
        compiler_params=pltpu.CompilerParams(
            collective_id=0, has_side_effects=True, vmem_limit_bytes=56 << 20
        ),
        name="krr_matvec",
    )
    out = call(
        points.T, charges.T, order, neighbours, neighbour_mask, leaf_skel, pair_skel, upper_skel
    )
    return out.T


def solution(mesh):
    placed = (P(("leaf", "sub"), None),) * 7 + (P(),)
    return jax.shard_map(
        shards, mesh=mesh, in_specs=placed, out_specs=P(("leaf", "sub"), None), check_vma=False
    )
```

time: 54.3 us -> 51.4 us (0.947)
  the two profiles are of different devices: /device:TPU:2 before, /device:TPU:1 now
where the time goes in v2:
time: 51.4 us; the launch traced here: 51.3 us
  Pallas kernels  49.8 us (97%)
  local copies, waits for them, and re-layouts  1.47 us (3%)
    pallas_call x1, Pallas kernels, shards(): call(points.T, charges.T, order, neighbours, neighbour_mask, leaf_skel, p...  49.8 us
    unnamed x1, local copies, waits for them, and re-layouts  1.47 us

profile of v2, /device:TPU:1, one launch (start us, length us, event | category | flops | bytes accessed | tf_op | source)
XLA Modules:
  0.0 51.3 jit_solution(3841198284279483914)
XLA Ops:
  0.0 49.8 %krr_matvec.1 = f32[16,1024]{1,0:T(8,128)} custom-call(f32[64,1024]{1,0:T(8,128)} %bitcast.4, f32[16,1024]{1,0:T(8,128)} %bitcast.5, s32[1,1024]{1,0:T(1,128)} %order_ref.1, s32[2,32]{1,0:T(2,128)} %nbr_ref.1, s32[2,32]{1,0:T(2,128)} %msk_ref.1, s32[2,128]{1,0:T(2,128)} %lsk_ref.1, s32[1,128]{1,0:T(1,128)} %psk_ref.1, s32[512,128]{1,0:T(8,128)} %usk_ref.1), custom_call_target="tpu_custom_call" | custom-call | tf_op jit(solution)/shard_map/krr_matvec/pallas_call | solution.py:399
  49.8 1.5 %copy.10 = f32[1024,16]{0,1:T(8,128)} copy(f32[1024,16]{0,1:T(8,128)} %bitcast.3) | data formatting | bytes 131072

commit v3 on v2

--- a/solution.py
+++ b/solution.py
@@ -79,12 +79,19 @@
     return jnp.dot(points, onehot(sel, points.shape[1]), preferred_element_type=F32).astype(BF16)
 
 
+def lookup(table, sel):
+    pad = jnp.zeros((6, table.shape[1]), F32)
+    rows = jnp.concatenate([(table >> 5).astype(F32), (table & 31).astype(F32), pad], axis=0)
+    found = jnp.dot(rows.astype(BF16), onehot(sel, table.shape[1]), preferred_element_type=F32)
+    return (found[0:1] * 32.0 + found[1:2]).astype(jnp.int32)
+
+
 def body(
     y_size, z_size,
     pts_ref, chg_ref, order_ref, nbr_ref, msk_ref, lsk_ref, psk_ref, usk_ref,
     out_ref,
-    win, own_swp, acc, cnt, tp, tu, n8, n4, n2, u4, u2, ups, crosses, downs, far, leaf_mats,
-    wsend, wrecv, psend, precv, usend, urecv,
+    win, own_swp, acc, cnt, tp, tu, n8, n4, n2, u4, u2, ups, crosses, downs, far, leaf_mats, tops, upper,
+    wsend, wrecv, psend, precv, usend, urecv, near_in, far_in,
 ):
     leaf = lax.axis_index("leaf")
     sub = lax.axis_index("sub")
@@ -93,8 +100,6 @@
     core = leaf % 2
     z = (leaf // 2) % z_size
     y = leaf // (2 * z_size)
-    prev = (leaf + leaf_count - 1) % leaf_count
-    nxt = (leaf + 1) % leaf_count
     partner = leaf + 1 - 2 * core
 
     def x_peer(step):
@@ -113,10 +118,44 @@
         [z_peer(s) for s in (4, 3, 5, 2, 6, 1, 7)],
         [y_peer(s) for s in (4, 3, 5, 2, 6, 1, 7)],
     ]
-    greet = stage_peers[2] + stage_peers[1] + stage_peers[0] + [(beyond, sub)]
     barrier = pltpu.get_barrier_semaphore()
-    for peer in greet:
-        pl.semaphore_signal(barrier, inc=1, device_id=peer, device_id_type=MESH)
+    own_chip = (leaf - core, leaf - core + 1)
+
+    def signal(semaphore, peer):
+        pl.semaphore_signal(semaphore, inc=1, device_id=peer, device_id_type=MESH)
+
+    for step in (1, 2, 3):
+        signal(barrier, (own_chip[0], (sub + step) % 4))
+
+    @pl.when(core == 1)
+    def _():
+        signal(barrier, (own_chip[0], sub))
+
+    for step in range(1, 8):
+        signal(barrier, ((y * z_size + (z + step) % z_size) * 2 + 1, sub))
+        signal(barrier, ((((y + step) % y_size) * z_size + z) * 2 + 1, sub))
+    signal(barrier, (beyond - beyond % 2 + 1, sub))
+
+    def group_entered():
+        @pl.when(core == 0)
+        def _():
+            pl.semaphore_wait(barrier, 7)
+            signal(near_in, (own_chip[1], sub))
+
+        @pl.when(core == 1)
+        def _():
+            pl.semaphore_wait(near_in, 1)
+
+    def far_entered():
+        @pl.when(core == 1)
+        def _():
+            pl.semaphore_wait(barrier, 2 * (z_size - 1) + 2 * (y_size - 1) + 2)
+            signal(far_in, (own_chip[0], sub))
+
+        @pl.when(core == 0)
+        def _():
+            pl.semaphore_wait(far_in, 1)
+
     place8 = [core * 4 + sub, z, y]
 
     def tree_copies(buffer, send_sem, recv_sem, stage):
@@ -149,26 +188,20 @@
     pts = pts_ref[...].astype(BF16)
     own_aug = augment(pts.astype(F32), 0.0)
     own_std = jnp.concatenate([pts, own_aug.astype(BF16)], axis=0)
-    coarse = (order // 32).astype(F32)
-    fine = (order % 32).astype(F32)
     skels = []
     for own in range(2):
-        part = slice(own * HALF, (own + 1) * HALF)
-        place = jnp.concatenate([coarse[:, part], fine[:, part], jnp.zeros((6, HALF), F32)], axis=0)
-        pick = onehot(lsk_ref[own : own + 1, :], HALF)
-        found = jnp.dot(place.astype(BF16), pick, preferred_element_type=F32)
-        where = (found[0:1] * 32.0 + found[1:2]).astype(jnp.int32)
+        where = lookup(order[:, own * HALF : (own + 1) * HALF], lsk_ref[own : own + 1, :])
         skels.append(choose(own_std, where))
     pair = jnp.concatenate(skels, axis=1)
     node = choose(pair, psk_ref[...])
     tp[0, pl.ds(place8[0], 1)] = node[None, 0:DIM]
 
-    pl.semaphore_wait(barrier, len(greet))
+    group_entered()
     tree_send(tp, psend, precv, 0)
 
     second = order[:, HALF:]
     grid = lax.dot_general(
-        onehot(second // 128, 8), onehot(second % 128, 128), NT, preferred_element_type=F32
+        onehot(second >> 7, 8), onehot(second & 127, 128), NT, preferred_element_type=F32
     )
     member = jnp.concatenate([grid[k : k + 1] for k in range(8)], axis=1)
     chg_hi, chg_lo = split2(chg_ref[...])
@@ -184,13 +217,14 @@
             device_id=peer, device_id_type=MESH,
         )
 
+    ours, theirs = 8 * core, 8 * (1 - core)
     sends = []
-    for step in (1, 3, 2):
-        sends.append(window_copy(4, 4 + (4 - step) % 4, step - 1, x_peer(step)))
-    sends.append(window_copy(4, 8, 3, (prev, sub)))
-    sends.append(window_copy(4, 0, 4, (nxt, sub)))
-    for copy in sends:
-        copy.start()
+
+    def window_send(*args):
+        sends.append(window_copy(*args))
+        sends[-1].start()
+
+    window_send(4, ours, 1, (partner, sub))
 
     def window_wait(slot):
         pltpu.make_async_copy(win.at[slot], win.at[slot], wrecv.at[slot]).wait()
@@ -206,6 +240,8 @@
         apply_mat(jnp.concatenate(weights, axis=1), pair_mat)
     )[None]
     tree_send(tu, usend, urecv, 0)
+    for step in (2, 1, 3):
+        window_send(4, 4 + (4 - step) % 4, 1 + step, x_peer(step))
 
     k = lax.broadcasted_iota(jnp.int32, (24, 32), 0)
     slot_k = k // 2
@@ -237,32 +273,50 @@
         mat = gauss(win[slot, 0:AUGD], own_swp[...]).astype(BF16)
         acc[...] += jnp.dot(rows, mat, preferred_element_type=F32)
 
+    firsts = [(256, 128, 64), (32, 16, 8), (4, 2, 0)]
+    bases = [device // 8, device // 64, 0 * device]
+
+    def chosen_rows(stage, depth):
+        count = 4 >> depth
+        start = firsts[stage][depth] + bases[stage] * count
+        return [usk_ref[pl.ds(start + j, 1), :] for j in range(count)]
+
+    def compose(stage):
+        at = [sel + 256 * j for j, sel in enumerate(chosen_rows(stage, 0))]
+        for depth in (1, 2):
+            at = [
+                lookup(jnp.concatenate(at[2 * j : 2 * j + 2], axis=1), sel)
+                for j, sel in enumerate(chosen_rows(stage, depth))
+            ]
+        tops[stage] = onehot(at[0], 8 * SKEL)
+
     def select_stage(stage):
-        firsts = [(256, 128, 64), (32, 16, 8), (4, 2, 0)][stage]
-        base = [device // 8, device // 64, 0 * device][stage]
         tree_wait(tp, precv, stage)
+        raw = [tp[stage, j] for j in range(8)]
+        if stage < 2:
+            wide = jnp.concatenate(raw, axis=1)
+            top = jnp.dot(wide, tops[stage], preferred_element_type=F32).astype(BF16)
+            tp[stage + 1, pl.ds(place8[stage + 1], 1)] = top[None]
+            if stage == 0:
+                far_entered()
+            tree_send(tp, psend, precv, stage + 1)
+            if stage == 0:
+                window_send(4, theirs, 0, (beyond, sub))
         nodes = []
         for j in range(8):
-            pts = tp[stage, j]
-            nodes.append(
-                jnp.concatenate([pts, augment(pts.astype(F32), 0.0).astype(BF16)], axis=0)
-            )
+            rows = augment(raw[j].astype(F32), 0.0).astype(BF16)
+            nodes.append(jnp.concatenate([raw[j], rows], axis=0))
             n8[stage, j] = nodes[-1]
-        for depth, kept in ((0, n4), (1, n2), (2, None)):
-            if depth == 2 and stage == 2:
-                break
-            count = len(nodes) // 2
-            pairs = [jnp.concatenate(nodes[2 * j : 2 * j + 2], axis=1) for j in range(count)]
-            nodes = []
-            for j in range(count):
-                sel = usk_ref[pl.ds(firsts[depth] + base * count + j, 1), :]
-                nodes.append(choose(pairs[j], sel))
-                if kept is not None:
-                    kept[stage, j] = nodes[-1]
+        for depth, kept in ((0, n4), (1, n2)):
+            sels = chosen_rows(stage, depth)
+            nodes = [
+                choose(jnp.concatenate(nodes[2 * j : 2 * j + 2], axis=1), sel)
+                for j, sel in enumerate(sels)
+            ]
+            for j, found in enumerate(nodes):
+                kept[stage, j] = found
         if stage < 2:
-            tp[stage + 1, pl.ds(place8[stage + 1], 1)] = nodes[0][None, 0:DIM]
-            tree_send(tp, psend, precv, stage + 1)
-            return nodes[0]
+            return choose(jnp.concatenate(nodes, axis=1), chosen_rows(stage, 2)[0])
         return None
 
     def pair_of(buffer, stage, j):
@@ -305,19 +359,27 @@
         far[3 * stage + 1] = apply_mat(u4[stage, b1], crosses[3 * stage + 1])
         far[3 * stage + 2] = apply_mat(u2[stage, c1], crosses[3 * stage + 2])
 
+    def way_down():
+        value = far[5]
+        for index in range(4, -1, -1):
+            value = far[index] + apply_mat(stack2(value), downs[index])
+        mat = downs[5].astype(F32)
+        for index in range(4, -1, -1):
+            mat = apply_mat(stack2(mat), downs[index])
+        mat = stack2(mat)
+        for own in range(2):
+            to_leaf, to_points = leaf_mats[own, :, PTS:], leaf_mats[own, :, 0:PTS]
+            term = far[9 + own] + apply_mat(stack2(value), to_leaf)
+            acc[own * RHS : (own + 1) * RHS] += apply_mat(stack2(term), to_points)
+            upper[own] = apply_mat(stack2(apply_mat(mat, to_leaf)), to_points).astype(BF16)
+
+    compose(0)
+    compose(1)
     near(4)
     top = select_stage(0)
     matrices(0, top)
     weights_stage(0)
 
-    relays = []
-    for i, dx in enumerate((1, 3, 2)):
-        window_wait(4 + dx)
-        relays.append(window_copy(4 + dx, 8 + dx, 5 + 2 * i, (prev, sub)))
-        relays.append(window_copy(4 + dx, dx, 6 + 2 * i, (nxt, sub)))
-        relays[-2].start()
-        relays[-1].start()
-
     def group_block(i, carry):
         near(4 + i)
         return carry
@@ -326,38 +388,47 @@
         return i + (i // 2) * (1 - 2 * (i % 2))
 
     def partner_block(i, carry):
-        slot = gray(i) + 8 * (1 - core)
+        slot = gray(i) + theirs
         window_wait(slot)
         near(slot)
         return carry
 
     def beyond_block(i, carry):
-        slot = gray(i) + 8 * core
+        slot = gray(i) + ours
         window_wait(slot)
         near(slot)
         return carry
 
+    window_wait(theirs)
+    near(theirs)
+    window_wait(ours)
+    near(ours)
+    for dx in (1, 3, 2):
+        window_wait(4 + dx)
+        window_send(4 + dx, theirs + dx, 4 + dx, (beyond, sub))
+        window_send(4 + dx, ours + dx, 7 + dx, (partner, sub))
     lax.fori_loop(1, 4, group_block, 0)
-    lax.fori_loop(0, 4, partner_block, 0)
     top = select_stage(1)
     matrices(1, top)
     weights_stage(1)
-    lax.fori_loop(0, 4, beyond_block, 0)
+    lax.fori_loop(1, 4, partner_block, 0)
+    way_down()
     select_stage(2)
     matrices(2, None)
     weights_stage(2)
+    lax.fori_loop(1, 4, beyond_block, 0)
 
     value = far[8]
-    for index in range(7, -1, -1):
+    for index in (7, 6):
         value = far[index] + apply_mat(stack2(value), downs[index])
+    stacked = stack2(value)
     for own in range(2):
-        term = far[9 + own] + apply_mat(stack2(value), leaf_mats[own, :, PTS:])
-        acc[own * RHS : (own + 1) * RHS] += apply_mat(stack2(term), leaf_mats[own, :, 0:PTS])
+        acc[own * RHS : (own + 1) * RHS] += apply_mat(stacked, upper[own])
 
     mine = win[4, DIM:AUGD].astype(F32)[3:4]
     out_ref[...] = jnp.where(mine > 0.5, acc[RHS:], acc[:RHS])
 
-    for copy in sends + relays + tree_sends:
+    for copy in sends + tree_sends:
         copy.wait_send()
 
 
@@ -384,12 +455,16 @@
             pltpu.VMEM((8, SKEL, SKEL), BF16),
             pltpu.VMEM((11, RHS, SKEL), F32),
             pltpu.VMEM((2, SKEL, PTS + SKEL), BF16),
+            pltpu.VMEM((2, 8 * SKEL, SKEL), BF16),
+            pltpu.VMEM((2, SKEL, PTS), BF16),
             pltpu.SemaphoreType.DMA((11,)),
             pltpu.SemaphoreType.DMA((12,)),
             pltpu.SemaphoreType.DMA((3, 7)),
             pltpu.SemaphoreType.DMA((3, 8)),
             pltpu.SemaphoreType.DMA((3, 7)),
             pltpu.SemaphoreType.DMA((3, 8)),
+            pltpu.SemaphoreType.REGULAR,
+            pltpu.SemaphoreType.REGULAR,
         ],
         compiler_params=pltpu.CompilerParams(
             collective_id=0, has_side_effects=True, vmem_limit_bytes=56 << 20

time: 51.4 us -> 48.1 us (0.936)
  the two profiles are of different devices: /device:TPU:1 before, /device:TPU:8 now
where the time goes in v3:
time: 48.1 us; the launch traced here: 47.9 us
  Pallas kernels  46.4 us (96%)
  local copies, waits for them, and re-layouts  1.47 us (3%)
    pallas_call x1, Pallas kernels, shards(): call(points.T, charges.T, order, neighbours, neighbour_mask, leaf_skel, p...  46.4 us
    unnamed x1, local copies, waits for them, and re-layouts  1.47 us

profile of v3, /device:TPU:8, one launch (start us, length us, event | category | flops | bytes accessed | tf_op | source)
XLA Modules:
  0.0 47.9 jit_solution(14989391482118555556)
XLA Ops:
  0.0 46.4 %krr_matvec.1 = f32[16,1024]{1,0:T(8,128)} custom-call(f32[64,1024]{1,0:T(8,128)} %bitcast.4, f32[16,1024]{1,0:T(8,128)} %bitcast.5, s32[1,1024]{1,0:T(1,128)} %order_ref.1, s32[2,32]{1,0:T(2,128)} %nbr_ref.1, s32[2,32]{1,0:T(2,128)} %msk_ref.1, s32[2,128]{1,0:T(2,128)} %lsk_ref.1, s32[1,128]{1,0:T(1,128)} %psk_ref.1, s32[512,128]{1,0:T(8,128)} %usk_ref.1), custom_call_target="tpu_custom_call" | custom-call | tf_op jit(solution)/shard_map/krr_matvec/pallas_call | solution.py:474
  46.4 1.5 %copy.10 = f32[1024,16]{0,1:T(8,128)} copy(f32[1024,16]{0,1:T(8,128)} %bitcast.3) | data formatting | bytes 131072

commit v4 on v3

--- a/solution.py
+++ b/solution.py
@@ -225,6 +225,8 @@
         sends[-1].start()
 
     window_send(4, ours, 1, (partner, sub))
+    for step in (1, 3):
+        window_send(4, 8 - step, 1 + step, x_peer(step))
 
     def window_wait(slot):
         pltpu.make_async_copy(win.at[slot], win.at[slot], wrecv.at[slot]).wait()
@@ -240,8 +242,8 @@
         apply_mat(jnp.concatenate(weights, axis=1), pair_mat)
     )[None]
     tree_send(tu, usend, urecv, 0)
-    for step in (2, 1, 3):
-        window_send(4, 4 + (4 - step) % 4, 1 + step, x_peer(step))
+    far_entered()
+    window_send(4, theirs, 0, (beyond, sub))
 
     k = lax.broadcasted_iota(jnp.int32, (24, 32), 0)
     slot_k = k // 2
@@ -297,11 +299,9 @@
             wide = jnp.concatenate(raw, axis=1)
             top = jnp.dot(wide, tops[stage], preferred_element_type=F32).astype(BF16)
             tp[stage + 1, pl.ds(place8[stage + 1], 1)] = top[None]
-            if stage == 0:
-                far_entered()
             tree_send(tp, psend, precv, stage + 1)
             if stage == 0:
-                window_send(4, theirs, 0, (beyond, sub))
+                window_send(4, 6, 3, x_peer(2))
         nodes = []
         for j in range(8):
             rows = augment(raw[j].astype(F32), 0.0).astype(BF16)
@@ -377,46 +377,52 @@
     compose(1)
     near(4)
     top = select_stage(0)
+    window_wait(theirs)
     matrices(0, top)
+    near(theirs)
     weights_stage(0)
 
     def group_block(i, carry):
-        near(4 + i)
+        near(5 + 2 * i)
         return carry
 
-    def gray(i):
-        return i + (i // 2) * (1 - 2 * (i % 2))
-
     def partner_block(i, carry):
-        slot = gray(i) + theirs
+        slot = theirs + 1 + 2 * i
         window_wait(slot)
         near(slot)
         return carry
 
     def beyond_block(i, carry):
-        slot = gray(i) + ours
+        slot = ours + 1 + 2 * i
         window_wait(slot)
         near(slot)
         return carry
 
-    window_wait(theirs)
-    near(theirs)
+    for dx in (1, 3):
+        window_wait(4 + dx)
+        window_send(4 + dx, ours + dx, 7 + dx, (partner, sub))
+    lax.fori_loop(0, 2, group_block, 0)
     window_wait(ours)
+    for step in (1, 3):
+        window_send(ours, ours + (4 - step), 4 + step // 2, x_peer(step))
     near(ours)
-    for dx in (1, 3, 2):
-        window_wait(4 + dx)
-        window_send(4 + dx, theirs + dx, 4 + dx, (beyond, sub))
-        window_send(4 + dx, ours + dx, 7 + dx, (partner, sub))
-    lax.fori_loop(1, 4, group_block, 0)
     top = select_stage(1)
+    window_wait(6)
+    window_send(6, theirs + 2, 6, (beyond, sub))
+    window_send(6, ours + 2, 9, (partner, sub))
     matrices(1, top)
+    near(6)
     weights_stage(1)
-    lax.fori_loop(1, 4, partner_block, 0)
+    lax.fori_loop(0, 2, partner_block, 0)
+    window_wait(theirs + 2)
+    near(theirs + 2)
     way_down()
+    lax.fori_loop(0, 2, beyond_block, 0)
     select_stage(2)
+    window_wait(ours + 2)
     matrices(2, None)
+    near(ours + 2)
     weights_stage(2)
-    lax.fori_loop(1, 4, beyond_block, 0)
 
     value = far[8]
     for index in (7, 6):

time: 48.1 us -> 41.2 us (0.86)
  the two profiles are of different devices: /device:TPU:8 before, /device:TPU:1 now
where the time goes in v4:
time: 41.2 us; the launch traced here: 40.5 us
  Pallas kernels  39 us (95%)
  local copies, waits for them, and re-layouts  1.47 us (4%)
    pallas_call x1, Pallas kernels, shards(): call(points.T, charges.T, order, neighbours, neighbour_mask, leaf_skel, p...  39 us
    unnamed x1, local copies, waits for them, and re-layouts  1.47 us

profile of v4, /device:TPU:1, one launch (start us, length us, event | category | flops | bytes accessed | tf_op | source)
XLA Modules:
  0.0 40.5 jit_solution(1165696183545317466)
XLA Ops:
  0.0 39.0 %krr_matvec.1 = f32[16,1024]{1,0:T(8,128)} custom-call(f32[64,1024]{1,0:T(8,128)} %bitcast.4, f32[16,1024]{1,0:T(8,128)} %bitcast.5, s32[1,1024]{1,0:T(1,128)} %order_ref.1, s32[2,32]{1,0:T(2,128)} %nbr_ref.1, s32[2,32]{1,0:T(2,128)} %msk_ref.1, s32[2,128]{1,0:T(2,128)} %lsk_ref.1, s32[1,128]{1,0:T(1,128)} %psk_ref.1, s32[512,128]{1,0:T(8,128)} %usk_ref.1), custom_call_target="tpu_custom_call" | custom-call | tf_op jit(solution)/shard_map/krr_matvec/pallas_call | solution.py:480
  39.0 1.5 %copy.10 = f32[1024,16]{0,1:T(8,128)} copy(f32[1024,16]{0,1:T(8,128)} %bitcast.3) | data formatting | bytes 131072

commit v5 on v4

--- a/solution.py
+++ b/solution.py
@@ -88,8 +88,9 @@
 
 def body(
     y_size, z_size,
-    pts_ref, chg_ref, order_ref, nbr_ref, msk_ref, lsk_ref, psk_ref, usk_ref,
+    pts_in, chg_in, order_in, nbr_in, msk_in, lsk_in, psk_in, usk_in,
     out_ref,
+    pts_ref, chg_ref, order_ref, nbr_ref, msk_ref, lsk_ref, psk_ref, usk_ref, fetched,
     win, own_swp, acc, cnt, tp, tu, n8, n4, n2, u4, u2, ups, crosses, downs, far, leaf_mats, tops, upper,
     wsend, wrecv, psend, precv, usend, urecv, near_in, far_in,
 ):
@@ -136,6 +137,18 @@
         signal(barrier, ((((y + step) % y_size) * z_size + z) * 2 + 1, sub))
     signal(barrier, (beyond - beyond % 2 + 1, sub))
 
+    fetches = [
+        pltpu.make_async_copy(source, target, fetched.at[i])
+        for i, (source, target) in enumerate(
+            (
+                (order_in, order_ref), (lsk_in, lsk_ref), (psk_in, psk_ref), (pts_in, pts_ref),
+                (chg_in, chg_ref), (nbr_in, nbr_ref), (msk_in, msk_ref), (usk_in, usk_ref),
+            )
+        )
+    ]
+    for copy in fetches:
+        copy.start()
+
     def group_entered():
         @pl.when(core == 0)
         def _():
@@ -184,6 +197,8 @@
                 buffer.at[stage, slot], buffer.at[stage, slot], recv_sem.at[stage, slot]
             ).wait()
 
+    for copy in fetches[:4]:
+        copy.wait()
     order = order_ref[...]
     pts = pts_ref[...].astype(BF16)
     own_aug = augment(pts.astype(F32), 0.0)
@@ -204,6 +219,8 @@
         onehot(second >> 7, 8), onehot(second & 127, 128), NT, preferred_element_type=F32
     )
     member = jnp.concatenate([grid[k : k + 1] for k in range(8)], axis=1)
+    for copy in fetches[4:]:
+        copy.wait()
     chg_hi, chg_lo = split2(chg_ref[...])
     row = lax.broadcasted_iota(jnp.int32, (AUG, PTS), 0)
     win[4, 0:DIM] = pts
@@ -225,8 +242,6 @@
         sends[-1].start()
 
     window_send(4, ours, 1, (partner, sub))
-    for step in (1, 3):
-        window_send(4, 8 - step, 1 + step, x_peer(step))
 
     def window_wait(slot):
         pltpu.make_async_copy(win.at[slot], win.at[slot], wrecv.at[slot]).wait()
@@ -242,9 +257,8 @@
         apply_mat(jnp.concatenate(weights, axis=1), pair_mat)
     )[None]
     tree_send(tu, usend, urecv, 0)
-    far_entered()
-    window_send(4, theirs, 0, (beyond, sub))
-
+    for step in (1, 3):
+        window_send(4, 8 - step, 1 + step, x_peer(step))
     k = lax.broadcasted_iota(jnp.int32, (24, 32), 0)
     slot_k = k // 2
     ids = ((leaf + slot_k // 4 - 1) * 4 + (sub + slot_k % 4) % 4) * 2 + k % 2
@@ -376,6 +390,8 @@
     compose(0)
     compose(1)
     near(4)
+    far_entered()
+    window_send(4, theirs, 0, (beyond, sub))
     top = select_stage(0)
     window_wait(theirs)
     matrices(0, top)
@@ -384,12 +400,6 @@
 
     def group_block(i, carry):
         near(5 + 2 * i)
-        return carry
-
-    def partner_block(i, carry):
-        slot = theirs + 1 + 2 * i
-        window_wait(slot)
-        near(slot)
         return carry
 
     def beyond_block(i, carry):
@@ -413,15 +423,17 @@
     matrices(1, top)
     near(6)
     weights_stage(1)
-    lax.fori_loop(0, 2, partner_block, 0)
-    window_wait(theirs + 2)
+    for dx in (1, 3, 2):
+        window_wait(theirs + dx)
+    near(theirs + 1)
+    near(theirs + 3)
     near(theirs + 2)
     way_down()
     lax.fori_loop(0, 2, beyond_block, 0)
+    window_wait(ours + 2)
+    near(ours + 2)
     select_stage(2)
-    window_wait(ours + 2)
     matrices(2, None)
-    near(ours + 2)
     weights_stage(2)
 
     value = far[8]
@@ -442,9 +454,18 @@
     call = pl.pallas_call(
         functools.partial(body, 8, 8),
         out_shape=jax.ShapeDtypeStruct((RHS, PTS), F32),
-        in_specs=[pl.BlockSpec(memory_space=pltpu.VMEM)] * 8,
+        in_specs=[pl.BlockSpec(memory_space=pl.ANY)] * 8,
         out_specs=pl.BlockSpec(memory_space=pltpu.VMEM),
         scratch_shapes=[
+            pltpu.VMEM((DIM, PTS), F32),
+            pltpu.VMEM((RHS, PTS), F32),
+            pltpu.VMEM(order.shape, jnp.int32),
+            pltpu.VMEM(neighbours.shape, jnp.int32),
+            pltpu.VMEM(neighbour_mask.shape, jnp.int32),
+            pltpu.VMEM(leaf_skel.shape, jnp.int32),
+            pltpu.VMEM(pair_skel.shape, jnp.int32),
+            pltpu.VMEM(upper_skel.shape, jnp.int32),
+            pltpu.SemaphoreType.DMA((8,)),
             pltpu.VMEM((12, WROWS, PTS), BF16),
             pltpu.VMEM((AUGD, PTS), BF16),
             pltpu.VMEM((2 * RHS, PTS), F32),

time: 41.2 us -> 40.4 us (0.981); the launches traced: 40.5 us -> 40.2 us
  no operation moved by 1% of the time
where the time goes in v5:
time: 40.4 us; the launch traced here: 40.2 us
  Pallas kernels  38.7 us (96%)
  local copies, waits for them, and re-layouts  1.47 us (4%)
    pallas_call x1, Pallas kernels, shards(): call(points.T, charges.T, order, neighbours, neighbour_mask, leaf_skel, p...  38.7 us
    unnamed x1, local copies, waits for them, and re-layouts  1.47 us

profile of v5, /device:TPU:1, one launch (start us, length us, event | category | flops | bytes accessed | tf_op | source)
XLA Modules:
  0.0 40.2 jit_solution(13485334860818298165)
XLA Ops:
  0.0 38.7 %krr_matvec.1 = f32[16,1024]{1,0:T(8,128)} custom-call(f32[64,1024]{1,0:T(8,128)} %bitcast.4, f32[16,1024]{1,0:T(8,128)} %bitcast.5, s32[1,1024]{1,0:T(1,128)} %order_in.1, s32[2,32]{1,0:T(2,128)} %nbr_in.1, s32[2,32]{1,0:T(2,128)} %msk_in.1, s32[2,128]{1,0:T(2,128)} %lsk_in.1, s32[1,128]{1,0:T(1,128)} %psk_in.1, s32[512,128]{1,0:T(8,128)} %usk_in.1), custom_call_target="tpu_custom_call" | custom-call | tf_op jit(solution)/shard_map/krr_matvec/pallas_call | solution.py:501
  38.7 1.5 %copy.10 = f32[1024,16]{0,1:T(8,128)} copy(f32[1024,16]{0,1:T(8,128)} %bitcast.3) | data formatting | bytes 131072

commit v6 on v5

--- a/solution.py
+++ b/solution.py
@@ -393,10 +393,10 @@
     far_entered()
     window_send(4, theirs, 0, (beyond, sub))
     top = select_stage(0)
+    matrices(0, top)
+    weights_stage(0)
     window_wait(theirs)
-    matrices(0, top)
     near(theirs)
-    weights_stage(0)
 
     def group_block(i, carry):
         near(5 + 2 * i)
@@ -414,15 +414,15 @@
     lax.fori_loop(0, 2, group_block, 0)
     window_wait(ours)
     for step in (1, 3):
-        window_send(ours, ours + (4 - step), 4 + step // 2, x_peer(step))
+        window_send(ours, ours + (4 - step), 7 - 2 * (step // 2), x_peer(step))
     near(ours)
     top = select_stage(1)
+    matrices(1, top)
+    weights_stage(1)
     window_wait(6)
     window_send(6, theirs + 2, 6, (beyond, sub))
     window_send(6, ours + 2, 9, (partner, sub))
-    matrices(1, top)
     near(6)
-    weights_stage(1)
     for dx in (1, 3, 2):
         window_wait(theirs + dx)
     near(theirs + 1)

time: 40.4 us -> 41.4 us (1.025)
  Pallas kernels: 38.7 us -> 39.7 us
    pallas_call x1, Pallas kernels: 38.7 us -> 39.7 us  [shards(): call(points.T, charges.T, order, neighbours, neighbour_mask, leaf_skel, p...]
where the time goes in v6:
time: 41.4 us; the launch traced here: 41.2 us
  Pallas kernels  39.7 us (96%)
  local copies, waits for them, and re-layouts  1.47 us (4%)
    pallas_call x1, Pallas kernels, shards(): call(points.T, charges.T, order, neighbours, neighbour_mask, leaf_skel, p...  39.7 us
    unnamed x1, local copies, waits for them, and re-layouts  1.47 us

profile of v6, /device:TPU:1, one launch (start us, length us, event | category | flops | bytes accessed | tf_op | source)
XLA Modules:
  0.0 41.2 jit_solution(3961366142107359396)
XLA Ops:
  0.0 39.7 %krr_matvec.1 = f32[16,1024]{1,0:T(8,128)} custom-call(f32[64,1024]{1,0:T(8,128)} %bitcast.4, f32[16,1024]{1,0:T(8,128)} %bitcast.5, s32[1,1024]{1,0:T(1,128)} %order_in.1, s32[2,32]{1,0:T(2,128)} %nbr_in.1, s32[2,32]{1,0:T(2,128)} %msk_in.1, s32[2,128]{1,0:T(2,128)} %lsk_in.1, s32[1,128]{1,0:T(1,128)} %psk_in.1, s32[512,128]{1,0:T(8,128)} %usk_in.1), custom_call_target="tpu_custom_call" | custom-call | tf_op jit(solution)/shard_map/krr_matvec/pallas_call | solution.py:501
  39.7 1.5 %copy.10 = f32[1024,16]{0,1:T(8,128)} copy(f32[1024,16]{0,1:T(8,128)} %bitcast.3) | data formatting | bytes 131072
